TPU v7x, 32 devices: a whole 2x2x4 slice. The times are simulated.
32 devices in a mesh: sub: 4 (over y, x), frow: 4 (over z), fcol: 2 (over core).
Axes of the slice: x: 2, y: 2, z: 4, core: 2. Of those that a mesh axis runs over, the one named last changes fastest.
Arguments:
- subgrids: float32 [128, 2, 512, 512], P('sub', None, ('frow', 'fcol')), may hold values from -0.01171875 to 0.01171875
- window: float32 [512, 512], P(('frow', 'fcol')), may hold values from 0.25 to 1
- counts: int32 [4], P('sub'), may hold values from 1 to 32, as said below
- nonempty: int32 [128], P('sub'), may hold values from -1 to 127, as said below
- column_u: int32 [1], replicated, may hold values from 0 to 65535
Outputs:
- facets: float32 [8, 2, 512, 8192], P('fcol', None, ('sub', 'frow'))
Inputs may be any that keep to these rules, and one draw needn't show every extreme that they name: counts[i] is how many of owner i's 32 slots hold a nonempty subgrid, always its first slots; one owner's count is 32 in every draw. `nonempty`: entries i*32 to (i+1)*32 - 1 belong to owner i; entry i*32+j for j below counts[i] is a distinct column position within i*32 to (i+1)*32 - 1, later entries are -1.
All inputs are finite; a program needn't handle non-finite values.
Results may differ from a plain program's by a relative error of at most 0.0003.
Values sent between devices are 32-bit elements; how exact they have to be, the bound alone decides.
A program may use at most 128 MiB of HBM per device.

v0:
```python
import math

import jax
import jax.numpy as jnp
from jax import lax
from jax.sharding import PartitionSpec as P

IMAGE = 65536
FACET = 8192
M = 512
ROW_DEV = 32


def twiddles(index):
    angle = index.astype(jnp.float32) * (2.0 * math.pi / IMAGE)
    return (jnp.cos(angle), jnp.sin(angle))


def dft_rows(weighted, position, v_start, row_ids):
    v_count = weighted.shape[1]
    v_ids = v_start + jnp.arange(v_count, dtype=jnp.int32) + jnp.maximum(position, 0) * M
    cos_part, sin_part = twiddles(row_ids[:, None] * v_ids[None, :] % IMAGE)
    left = jnp.concatenate(
        [jnp.concatenate([cos_part, -sin_part], 1), jnp.concatenate([sin_part, cos_part], 1)], 0
    )
    right = weighted.reshape(2 * v_count, weighted.shape[2])
    product = jnp.dot(
        left, right, precision=lax.Precision.HIGHEST, preferred_element_type=jnp.float32
    )
    return product.reshape(2, row_ids.shape[0], weighted.shape[2])


def local(subgrids, window, counts, nonempty, column_u):
    n_owners = lax.axis_size("sub")
    row_total = ROW_DEV * n_owners * lax.axis_size("frow")
    v_count = subgrids.shape[2]
    v_start = lax.axis_index(("frow", "fcol")) * v_count
    row_ids = jnp.arange(row_total, dtype=jnp.int32)
    start_sum = jnp.zeros((2, row_ids.shape[0], subgrids.shape[3]), jnp.float32)

    def add_slot(slot_data, position, running):
        weighted = slot_data * window[None]
        return running + dft_rows(weighted, position, v_start, row_ids)

    def add_owned(step, running):
        return add_slot(subgrids[step], nonempty[step], running)

    partial_sum = lax.fori_loop(0, counts[0], add_owned, start_sum)
    own_rows = lax.psum_scatter(
        partial_sum, ("sub", "frow", "fcol"), scatter_dimension=1, tiled=True
    )
    pair_sum = lax.all_gather(own_rows, "fcol", axis=1, tiled=True)
    n_local = IMAGE // FACET // lax.axis_size("fcol")
    facet_ids = lax.axis_index("fcol") * n_local + jnp.arange(n_local, dtype=jnp.int32)
    u_ids = (jnp.arange(M, dtype=jnp.int32) + column_u[0]) % IMAGE
    base_ids = FACET * u_ids % IMAGE
    cos_facet, sin_facet = twiddles(facet_ids[:, None] * base_ids[None, :] % IMAGE)
    rot_real = pair_sum[0][None] * cos_facet[:, None, :] - pair_sum[1][None] * sin_facet[:, None, :]
    rot_imag = pair_sum[0][None] * sin_facet[:, None, :] + pair_sum[1][None] * cos_facet[:, None, :]
    left = jnp.stack(
        [jnp.concatenate([rot_real, -rot_imag], -1), jnp.concatenate([rot_imag, rot_real], -1)], 1
    )
    cos_col, sin_col = twiddles(
        u_ids[:, None] * jnp.arange(FACET, dtype=jnp.int32)[None, :] % IMAGE
    )
    right = jnp.concatenate([cos_col, sin_col], 0)
    pair_count = pair_sum.shape[1]
    result = jnp.dot(
        left.reshape(n_local * 2 * pair_count, 2 * M),
        right,
        precision=lax.Precision.HIGHEST,
        preferred_element_type=jnp.float32,
    )
    return result.reshape(n_local, 2, pair_count, FACET)


def solution(mesh):
    return jax.shard_map(
        local,
        mesh=mesh,
        in_specs=(
            P("sub", None, ("frow", "fcol"), None),
            P(("frow", "fcol"), None),
            P("sub"),
            P("sub"),
            P(),
        ),
        out_specs=P("fcol", None, ("sub", "frow"), None),
        check_vma=False,
    )
```

profile of v0, /device:TPU:0, one launch (start us, length us, event | category | flops | bytes accessed | tf_op | source)
XLA Modules:
  0.0 414.9 jit_solution(14862729356159703816)
XLA Ops:
  6.8 70.9 %while.13 = (s32[]{:T(128)}, f32[2,512,512]{2,1,0:T(8,128)S(1)}, s32[]{:T(128)}, s32[]{:T(128)}, s32[32]{0:T(128)}, /*index=5*/f32[32,2,64,512]{3,2,1,0:T(8,128)...) while((s32[]{:T(128)}, f32[2,512,512]{2,1,0:T(8,128)S(1)}, ...), condition=%wide.region_1.2_spmd.clone, body=%wide.region_0.1_spmd.clone.sunk | while | flops 806781056 | bytes 6947535 | solution.py:48
  7.5 1.3 dynamic_slice.18
  10.4 1.0 fusion.41
  11.7 2.2 convolution_add_fusion.2
  14.5 1.3 dynamic_slice.18
  17.4 1.0 fusion.41
  18.7 2.2 convolution_add_fusion.2
  21.5 1.3 dynamic_slice.18
  24.5 1.0 fusion.41
  25.7 2.2 convolution_add_fusion.2
  28.5 1.3 dynamic_slice.18
  31.5 1.0 fusion.41
  32.7 2.2 convolution_add_fusion.2
  35.6 1.3 dynamic_slice.18
  38.5 1.0 fusion.41
  39.8 2.2 convolution_add_fusion.2
  42.6 1.3 dynamic_slice.18
  45.5 1.0 fusion.41
  46.8 2.2 convolution_add_fusion.2
  49.6 1.3 dynamic_slice.18
  53.8 2.2 convolution_add_fusion.2
  56.6 1.3 dynamic_slice.18
  60.8 2.2 convolution_add_fusion.2
  63.7 1.3 dynamic_slice.18
  67.9 2.2 convolution_add_fusion.2
  70.7 1.3 dynamic_slice.18
  74.9 2.2 convolution_add_fusion.2
  77.7 1.3 copy-done
  79.9 69.3 %fusion.21 = (f32[512,8192]{1,0:T(8,128)}, f32[512,8192]{1,0:T(8,128)}) fusion(s32[512]{0:T(512)S(1)} %get-tuple-element.157), kind=kLoop, calls=%fused_computation.32 | loop fusion | flops 58720256 | bytes 33556480 | tf_op jit(solution)/shard_map/cos | solution.py:16
  149.2 222.7 %reduce-scatter.2.cloned.1.call-done = f32[2,16,512]{2,1,0:T(8,128)} async-done(((f32[2,512,512]{2,1,0:T(8,128)}), f32[2,16,512]{2,1,0:T(8,128)}) %reduce-scatter.2.cloned.1.call-update) | async-done | bytes 65552 | tf_op jit(solution)/shard_map/reduce_scatter | solution.py:49
  371.9 2.4 all_gather.3
  374.5 33.5 %fusion.11 = f32[4,2,32,8192]{3,2,1,0:T(8,128)} fusion(f32[512,8192]{1,0:T(8,128)} %get-tuple-element.155, f32[512,8192]{1,0:T(8,128)} %get-tuple-element.154, f32[4,1,32,1024]{3,2,1,0:T(8,128)S(1)} %get-tuple-element.146, f32[4,1,32,1024]{3,2,1,0:T(8,128)S(1)} %get-tuple-element.145), kind=kOutput, calls=%fused_computation.19 | convolution fusion | flops 25778454528 | bytes 42991616 | tf_op jit(solution)/shard_map/dot_general | solution.py:68
  (44 shorter events, 17.1 us)
Async XLA Ops:
  6.5 365.3 %reduce-scatter.2.cloned.1.call-start = ((), (), s32[]{:S(2)}) async-start(), calls=%async_computation.1 | async-start | bytes 2162688 | tf_op jit(solution)/shard_map/reduce_scatter | solution.py:49
  77.7 1.3 copy-start
Sparse Core Ops, SparseCore 0:
  79.2 292.6 reduce-scatter.1
where the time goes:
time: 417 us; the launch traced here: 415 us
  waiting for transfers between devices  223 us (53%)
  other arithmetic  92.5 us (22%)
  matrix products  55 us (13%)
  local copies, waits for them, and re-layouts  14.2 us (3%)
  between operations  14.1 us (3%)
  loops' own time  14 us (3%)
    reduce_scatter x1, waiting for transfers between devices, local(): lax.psum_scatter(partial_sum, ('sub', 'frow', 'fcol'), scatter_dimension=...  223 us
    cos x2, other arithmetic, twiddles(): return (jnp.cos(angle), jnp.sin(angle))  69.5 us
    dot_general x1, matrix products, local(): jnp.dot(left.reshape(n_local * 2 * pair_count, 2 * M), right, precision=l...  33.5 us
    dot_general x10, matrix products, dft_rows(): jnp.dot(left, right, precision=lax.Precision.HIGHEST, preferred_element_t...  21.5 us
    another operation x1, loops' own time, local(): partial_sum = lax.fori_loop(0, counts[0], add_owned, start_sum)  14 us
    dynamic_slice x10, local copies, waits for them, and re-layouts, add_owned(): return add_slot(subgrids[step], nonempty[step], running)  12.7 us
    neg x10, other arithmetic, dft_rows(): -sin_part  10.5 us
    mul x10, other arithmetic, add_slot(): weighted = slot_data * window[None]  10.2 us
  transfers between devices with their start and end apart: 1, of which 1 were waited for; matrix products, arithmetic and copies ran while one was open for 17% of the time, Pallas kernels for 0%

commit v1 on v0

v1 whole, which is shorter than its diff:
```python
import functools
import math

import jax
import jax.numpy as jnp
from jax import lax
from jax.experimental import pallas as pl
from jax.experimental.pallas import tpu as pltpu
from jax.sharding import PartitionSpec as P

IMAGE = 65536
FACET = 8192
M = 512
ROW_DEV = 32
LANES = 128
VMEM_BYTES = 56 * 1024 * 1024


def sincos(k):
    q = (k + 16384) >> 15
    y = (k - (q << 15)).astype(jnp.float32) * (math.pi / IMAGE)
    z = y * y
    c = 1.0 + z * (-1.0 / 2 + z * (1.0 / 24 + z * (-1.0 / 720 + z * (1.0 / 40320))))
    s = y * (1.0 + z * (-1.0 / 6 + z * (1.0 / 120 + z * (-1.0 / 5040))))
    swap = (q & 1) == 1
    cos_part = jnp.where(swap, s, c)
    sin_part = jnp.where(swap, c, s)
    cos_part = jnp.where(((q + 1) & 2) != 0, -cos_part, cos_part)
    sin_part = jnp.where((q & 2) != 0, -sin_part, sin_part)
    return cos_part, sin_part


def split(x):
    high = x.astype(jnp.bfloat16)
    low = (x - high.astype(jnp.float32)).astype(jnp.bfloat16)
    return high, low


def column_kernel(group, start_ref, count_ref, pos_ref, sub_ref, win_ref, out_ref, left, rot, xs, acc):
    cap, _, v_count, _ = sub_ref.shape
    rows = out_ref.shape[1]
    half = rows // 2
    depth = group * v_count
    n_groups = (count_ref[0] + group - 1) // group

    @pl.when(pl.program_id(0) == 0)
    def _():
        def one_slot(slot, carry):
            v = lax.broadcasted_iota(jnp.int32, (v_count, LANES), 0) + start_ref[0]
            n = v + M * jnp.maximum(pos_ref[slot], 0)
            cos_part, sin_part = sincos((rows - 1) * n)
            live = jnp.where(slot < count_ref[0], 1.0, 0.0)
            rot[slot, 0] = cos_part * live
            rot[slot, 1] = sin_part * live
            return carry

        lax.fori_loop(0, n_groups * group, one_slot, 0)
        step = 32

        def one_block(item, carry):
            g = item // (half // step)
            r = item % (half // step)
            lane = lax.broadcasted_iota(jnp.int32, (1, depth), 1)
            slot_of = lane // v_count
            p = jnp.zeros((1, depth), jnp.int32)
            for s in range(group):
                p = jnp.where(slot_of == s, jnp.maximum(pos_ref[g * group + s], 0), p)
            n = lane % v_count + start_ref[0] + M * p
            d = lax.broadcasted_iota(jnp.int32, (step, 1), 0) + r * step
            cos_part, sin_part = sincos((2 * d + 1) * n)
            for part, base in ((cos_part, 0), (sin_part, half)):
                high, low = split(part)
                here = pl.ds(pl.multiple_of(base + r * step, step), step)
                left[g, here, 0:depth] = high
                left[g, here, depth : 2 * depth] = low
                left[g, here, 2 * depth : 3 * depth] = high
            return carry

        lax.fori_loop(0, n_groups * (half // step), one_block, 0)

    acc[...] = jnp.zeros_like(acc)

    def one_group(g, carry):
        for s in range(group):
            slot = g * group + s
            wc = win_ref[...] * rot[slot, 0]
            ws = win_ref[...] * rot[slot, 1]
            xr, xi = sub_ref[slot, 0], sub_ref[slot, 1]
            x = jnp.concatenate([xr * wc - xi * ws, xr * ws + xi * wc], 1)
            high, low = split(x)
            xs[s * v_count : (s + 1) * v_count, :] = high
            xs[depth + s * v_count : depth + (s + 1) * v_count, :] = low
        high = xs[0:depth, :]
        right = jnp.concatenate([high, high, xs[depth : 2 * depth, :]], 0)
        acc[...] += jnp.dot(left[g], right, preferred_element_type=jnp.float32)
        return carry

    lax.fori_loop(0, n_groups, one_group, 0)
    n_low = half // ROW_DEV
    for k in range(n_low):
        d = slice(k * ROW_DEV, (k + 1) * ROW_DEV)
        e = slice(half + k * ROW_DEV, half + (k + 1) * ROW_DEV)
        cr, ci = acc[d, :LANES], acc[d, LANES:]
        sr, si = acc[e, :LANES], acc[e, LANES:]
        out_ref[0, e, :] = cr - si
        out_ref[1, e, :] = sr + ci
        lower = slice((n_low - 1 - k) * ROW_DEV, (n_low - k) * ROW_DEV)
        out_ref[0, lower, :] = cr + si
        out_ref[1, lower, :] = ci - sr


def column_partial(subgrids, window, counts, nonempty, v_start, rows):
    cap, _, v_count, width = subgrids.shape
    group = min(8, cap)
    depth = group * v_count
    flops = 2 * rows * 2 * width * cap * v_count * 3
    return pl.pallas_call(
        functools.partial(column_kernel, group),
        grid=(width // LANES,),
        out_shape=jax.ShapeDtypeStruct((2, rows, width), jnp.float32),
        in_specs=[
            pl.BlockSpec(memory_space=pltpu.SMEM),
            pl.BlockSpec(memory_space=pltpu.SMEM),
            pl.BlockSpec(memory_space=pltpu.SMEM),
            pl.BlockSpec((cap, 2, v_count, LANES), lambda t: (0, 0, 0, t)),
            pl.BlockSpec((v_count, LANES), lambda t: (0, t)),
        ],
        out_specs=pl.BlockSpec((2, rows, LANES), lambda t: (0, 0, t)),
        scratch_shapes=[
            pltpu.VMEM((cap // group, rows, 3 * depth), jnp.bfloat16),
            pltpu.VMEM((cap, 2, v_count, LANES), jnp.float32),
            pltpu.VMEM((2 * depth, 2 * LANES), jnp.bfloat16),
            pltpu.VMEM((rows, 2 * LANES), jnp.float32),
        ],
        compiler_params=pltpu.CompilerParams(vmem_limit_bytes=VMEM_BYTES),
        cost_estimate=pl.CostEstimate(flops=flops, bytes_accessed=12 << 20, transcendentals=0),
        name="column_sum",
    )(v_start, counts, nonempty, subgrids, window)


TILE = 512


def reverse_lanes(x):
    index = (LANES - 1) - lax.broadcasted_iota(jnp.int32, (x.shape[0], LANES), 1)
    n = x.shape[1] // LANES
    parts = [
        jnp.take_along_axis(x[:, (n - 1 - i) * LANES : (n - i) * LANES], index, axis=1)
        for i in range(n)
    ]
    return jnp.concatenate(parts, 1)


def facet_kernel(n_local, meta_ref, sum_ref, out_ref, left, base, right, buf, sem):
    t = pl.program_id(0)
    steps = pl.num_programs(0)
    column = meta_ref[0]
    first = meta_ref[1]
    rows = sum_ref.shape[1]
    mid = FACET // 2

    @pl.when(t == 0)
    def _():
        u = lax.broadcasted_iota(jnp.int32, (1, M), 1)
        w = (u + column) & (IMAGE - 1)
        for j in range(n_local):
            cos_part, sin_part = sincos((2 * FACET * (first + j) + FACET - 1) * w)
            re, im = sum_ref[0], sum_ref[1]
            for part, value in ((0, re * cos_part - im * sin_part), (1, re * sin_part + im * cos_part)):
                high, low = split(value)
                here = slice((2 * j + part) * rows, (2 * j + part + 1) * rows)
                left[here, 0:M] = high
                left[here, M : 2 * M] = low
                left[here, 2 * M : 3 * M] = high

        def one_block(i, carry):
            here = pl.ds(pl.multiple_of(i * 16, 16), 16)
            w = (lax.broadcasted_iota(jnp.int32, (16, 1), 0) + i * 16 + column) & (IMAGE - 1)
            d = lax.broadcasted_iota(jnp.int32, (1, TILE), 1)
            cos_part, sin_part = sincos((2 * d + 1) * w)
            base[0, here, :] = cos_part
            base[1, here, :] = sin_part
            return carry

        lax.fori_loop(0, M // 16, one_block, 0)

    def one_block(i, carry):
        here = pl.ds(pl.multiple_of(i * 16, 16), 16)
        low_here = pl.ds(pl.multiple_of(M + i * 16, 16), 16)
        w = (lax.broadcasted_iota(jnp.int32, (16, LANES), 0) + i * 16 + column) & (IMAGE - 1)
        tc, ts = sincos((2 * TILE * t) * w)
        for k in range(TILE // LANES):
            lanes = slice(k * LANES, (k + 1) * LANES)
            bc, bs = base[0, here, lanes], base[1, here, lanes]
            high, low = split(bc * tc - bs * ts)
            right[here, lanes] = high
            right[low_here, lanes] = low
            lanes = slice(TILE + k * LANES, TILE + (k + 1) * LANES)
            high, low = split(bc * ts + bs * tc)
            right[here, lanes] = high
            right[low_here, lanes] = low
        return carry

    lax.fori_loop(0, M // 16, one_block, 0, unroll=2)
    slot = lax.rem(t, 2)

    def copies(step, place):
        upper = pltpu.make_async_copy(
            buf.at[place, 0],
            out_ref.at[:, :, :, pl.ds(pl.multiple_of(mid + step * TILE, TILE), TILE)],
            sem.at[place, 0],
        )
        lower = pltpu.make_async_copy(
            buf.at[place, 1],
            out_ref.at[:, :, :, pl.ds(pl.multiple_of(mid - (step + 1) * TILE, TILE), TILE)],
            sem.at[place, 1],
        )
        return upper, lower

    @pl.when(t >= 2)
    def _():
        for copy in copies(t - 2, slot):
            copy.wait()

    high = right[0:M, :]
    both = jnp.concatenate([high, high, right[M : 2 * M, :]], 0)
    for j in range(n_local):
        here = slice(2 * j * rows, 2 * (j + 1) * rows)
        product = jnp.dot(left[here, :], both, preferred_element_type=jnp.float32)
        rc, rs = product[:rows, :TILE], product[:rows, TILE:]
        ic, is_ = product[rows:, :TILE], product[rows:, TILE:]
        buf[slot, 0, j, 0] = rc - is_
        buf[slot, 0, j, 1] = rs + ic
        buf[slot, 1, j, 0] = reverse_lanes(rc + is_)
        buf[slot, 1, j, 1] = reverse_lanes(ic - rs)
    for copy in copies(t, slot):
        copy.start()

    @pl.when(t == steps - 1)
    def _():
        for copy in copies(t - 1, 1 - slot):
            copy.wait()
        for copy in copies(t, slot):
            copy.wait()


def facet_rows(column_sum, meta, n_local):
    rows = column_sum.shape[1]
    flops = 2 * (2 * n_local * rows) * (3 * M) * FACET
    return pl.pallas_call(
        functools.partial(facet_kernel, n_local),
        grid=(FACET // 2 // TILE,),
        out_shape=jax.ShapeDtypeStruct((n_local, 2, rows, FACET), jnp.float32),
        in_specs=[
            pl.BlockSpec(memory_space=pltpu.SMEM),
            pl.BlockSpec((2, rows, M), lambda t: (0, 0, 0)),
        ],
        out_specs=pl.BlockSpec(memory_space=pl.ANY),
        scratch_shapes=[
            pltpu.VMEM((2 * n_local * rows, 3 * M), jnp.bfloat16),
            pltpu.VMEM((2, M, TILE), jnp.float32),
            pltpu.VMEM((2 * M, 2 * TILE), jnp.bfloat16),
            pltpu.VMEM((2, 2, n_local, 2, rows, TILE), jnp.float32),
            pltpu.SemaphoreType.DMA((2, 2)),
        ],
        compiler_params=pltpu.CompilerParams(vmem_limit_bytes=VMEM_BYTES),
        cost_estimate=pl.CostEstimate(flops=flops, bytes_accessed=9 << 20, transcendentals=0),
        name="facet_rows",
    )(meta, column_sum)


def local(subgrids, window, counts, nonempty, column_u):
    n_blocks = lax.axis_size("sub") * lax.axis_size("frow")
    rows = ROW_DEV * n_blocks
    v_start = lax.axis_index(("frow", "fcol")) * subgrids.shape[2]
    partial_sum = column_partial(
        subgrids, window, counts, nonempty, v_start.astype(jnp.int32).reshape(1), rows
    )
    own_rows = lax.psum_scatter(
        partial_sum, ("sub", "frow", "fcol"), scatter_dimension=1, tiled=True
    )
    pair_sum = lax.all_gather(own_rows, "fcol", axis=1, tiled=True)
    block = lax.axis_index(("sub", "frow"))
    pair_sum = jnp.where(block < n_blocks // 2, jnp.flip(pair_sum, 1), pair_sum)
    n_local = IMAGE // FACET // lax.axis_size("fcol")
    meta = jnp.stack([column_u[0], (lax.axis_index("fcol") * n_local).astype(jnp.int32)])
    return facet_rows(pair_sum, meta, n_local)


def solution(mesh):
    return jax.shard_map(
        local,
        mesh=mesh,
        in_specs=(
            P("sub", None, ("frow", "fcol"), None),
            P(("frow", "fcol"), None),
            P("sub"),
            P("sub"),
            P(),
        ),
        out_specs=P("fcol", None, ("sub", "frow"), None),
        check_vma=False,
    )
```

time: 417 us -> 206 us (0.49)
  other arithmetic: 92.5 us -> 1.33 us
  waiting for transfers between devices: 223 us -> 148 us
  matrix products: 55 us -> 0 us
  Pallas kernels: 0 us -> 39.8 us
  local copies, waits for them, and re-layouts: 14.2 us -> 0.09 us
  loops' own time: 14 us -> 0 us
    reduce_scatter x1, waiting for transfers between devices: 223 us -> 148 us  [local(): lax.psum_scatter(partial_sum, ('sub', 'frow', 'fcol'), scatter_dimension=...]
    cos x2 -> x0, other arithmetic: 69.5 us -> none  [twiddles(): return (jnp.cos(angle), jnp.sin(angle))]
    dot_general x11 -> x0, matrix products: 55 us -> none  [the longest x1 33.5 us: local(): jnp.dot(left.reshape(n_local * 2 * pair_count, 2 * M), right, precision=l...]
    pallas_call x0 -> x2, Pallas kernels: none -> 39.8 us  [the longest x1 31.9 us: facet_rows(): pl.pallas_call(functools.partial(facet_kernel, n_local), grid=(FACET // 2...]
    another operation x1 -> x0, loops' own time: 14 us -> none  [local(): partial_sum = lax.fori_loop(0, counts[0], add_owned, start_sum)]
    dynamic_slice x10 -> x0, local copies, waits for them, and re-layouts: 12.7 us -> none  [add_owned(): return add_slot(subgrids[step], nonempty[step], running)]
    neg x11 -> x0, other arithmetic: 10.6 us -> none  [the longest x10 10.5 us: dft_rows(): -sin_part]
    mul x10 -> x0, other arithmetic: 10.2 us -> none  [add_slot(): weighted = slot_data * window[None]]
  transfers between devices with their start and end apart: 1 -> 1, of which waited for: 1 -> 1; matrix products, arithmetic and copies ran while one was open for 17% -> 0% of each run, Pallas kernels for 0% -> 0%
where the time goes in v1:
time: 206 us
  waiting for transfers between devices  148 us (72%)
  Pallas kernels  39.8 us (19%)
  between operations  14.7 us (7%)
  blocking collectives  2.24 us (1%)
    reduce_scatter x1, waiting for transfers between devices, local(): lax.psum_scatter(partial_sum, ('sub', 'frow', 'fcol'), scatter_dimension=...  148 us
    pallas_call x1, Pallas kernels, facet_rows(): pl.pallas_call(functools.partial(facet_kernel, n_local), grid=(FACET // 2...  31.9 us
    pallas_call x1, Pallas kernels, column_partial(): pl.pallas_call(functools.partial(column_kernel, group), grid=(width // LA...  7.94 us
  transfers between devices with their start and end apart: 1, of which 1 were waited for; matrix products, arithmetic and copies ran while one was open for 0% of the time, Pallas kernels for 0%

profile of v1, /device:TPU:0, one launch (start us, length us, event | category | flops | bytes accessed | tf_op | source)
XLA Modules:
  0.0 206.5 jit_solution(6533390699941871798)
XLA Ops:
  6.5 0.0 reduce-scatter.2.cloned.1.call-start
  7.2 7.9 %column_sum.1 = f32[2,512,512]{2,1,0:T(8,128)} custom-call(s32[1]{0:T(128)} %bitcast.1.start_ref, s32[1]{0:T(128)S(6)} %copy.6.count_ref, s32[32]{0:T(128)} %pos_ref.1, f32[32,2,64,512]{3,2,1,0:T(8,128)} %sub_ref.1, f32[64,512]{1,0:T(8,128)} %win_ref.1), custom_call_target="tpu_custom_call" | custom-call | flops 6442450944 | bytes 12582912 | tf_op jit(solution)/shard_map/column_sum/pallas_call | solution.py:117
  15.1 0.0 reduce-scatter.2.cloned.1.call-update
  15.8 0.7 pad_add_fusion.meta_ref
  16.5 148.3 %reduce-scatter.2.cloned.1.call-done = f32[2,16,512]{2,1,0:T(8,128)} async-done(((f32[2,512,512]{2,1,0:T(8,128)}), f32[2,16,512]{2,1,0:T(8,128)}) %reduce-scatter.2.cloned.1.call-update) | async-done | bytes 65552 | tf_op jit(solution)/shard_map/reduce_scatter | solution.py:279
  164.7 2.2 %all_gather.3 = f32[2,32,512]{2,1,0:T(8,128)S(1)} all-gather(f32[2,16,512]{2,1,0:T(8,128)} %reduce-scatter.2.cloned.1.call-done), channel_id=1, replica_groups=mesh['sub'=4,'frow'=4,'fcol'=2] {'fcol'}, dimensions={1}, use_global_device_ids=true | all-gather | bytes 196608 | tf_op jit(solution)/shard_map/all_gather | solution.py:282
  167.0 0.1 rev.4
  167.1 0.7 broadcast_select_fusion.sum_ref
  167.7 31.9 %facet_rows.1 = f32[4,2,32,8192]{3,2,1,0:T(8,128)} custom-call(s32[2]{0:T(128)} %pad_add_fusion.meta_ref, f32[2,32,512]{2,1,0:T(8,128)} %broadcast_select_fusion.sum_ref), custom_call_target="tpu_custom_call" | custom-call | flops 6442450944 | bytes 9437184 | tf_op jit(solution)/shard_map/facet_rows/pallas_call | solution.py:250
Async XLA Ops:
  6.5 158.2 %reduce-scatter.2.cloned.1.call-start = ((), (), s32[]{:S(2)}) async-start(), calls=%async_computation.1 | async-start | bytes 2162688 | tf_op jit(solution)/shard_map/reduce_scatter | solution.py:279
Sparse Core Ops, SparseCore 0:
  15.3 149.4 reduce-scatter.1

commit v2 on v1

--- a/solution.py
+++ b/solution.py
@@ -38,7 +38,7 @@
 
 def column_kernel(group, start_ref, count_ref, pos_ref, sub_ref, win_ref, out_ref, left, rot, xs, acc):
     cap, _, v_count, _ = sub_ref.shape
-    rows = out_ref.shape[1]
+    rows = out_ref.shape[2]
     half = rows // 2
     depth = group * v_count
     n_groups = (count_ref[0] + group - 1) // group
@@ -102,11 +102,11 @@
         e = slice(half + k * ROW_DEV, half + (k + 1) * ROW_DEV)
         cr, ci = acc[d, :LANES], acc[d, LANES:]
         sr, si = acc[e, :LANES], acc[e, LANES:]
-        out_ref[0, e, :] = cr - si
-        out_ref[1, e, :] = sr + ci
+        out_ref[0, 0, e, :] = cr - si
+        out_ref[0, 1, e, :] = sr + ci
         lower = slice((n_low - 1 - k) * ROW_DEV, (n_low - k) * ROW_DEV)
-        out_ref[0, lower, :] = cr + si
-        out_ref[1, lower, :] = ci - sr
+        out_ref[0, 0, lower, :] = cr + si
+        out_ref[0, 1, lower, :] = ci - sr
 
 
 def column_partial(subgrids, window, counts, nonempty, v_start, rows):
@@ -117,7 +117,7 @@
     return pl.pallas_call(
         functools.partial(column_kernel, group),
         grid=(width // LANES,),
-        out_shape=jax.ShapeDtypeStruct((2, rows, width), jnp.float32),
+        out_shape=jax.ShapeDtypeStruct((width // LANES, 2, rows, LANES), jnp.float32),
         in_specs=[
             pl.BlockSpec(memory_space=pltpu.SMEM),
             pl.BlockSpec(memory_space=pltpu.SMEM),
@@ -125,7 +125,7 @@
             pl.BlockSpec((cap, 2, v_count, LANES), lambda t: (0, 0, 0, t)),
             pl.BlockSpec((v_count, LANES), lambda t: (0, t)),
         ],
-        out_specs=pl.BlockSpec((2, rows, LANES), lambda t: (0, 0, t)),
+        out_specs=pl.BlockSpec((1, 2, rows, LANES), lambda t: (t, 0, 0, 0)),
         scratch_shapes=[
             pltpu.VMEM((cap // group, rows, 3 * depth), jnp.bfloat16),
             pltpu.VMEM((cap, 2, v_count, LANES), jnp.float32),
@@ -224,9 +224,9 @@
 
     high = right[0:M, :]
     both = jnp.concatenate([high, high, right[M : 2 * M, :]], 0)
+    products = jnp.dot(left[...], both, preferred_element_type=jnp.float32)
     for j in range(n_local):
-        here = slice(2 * j * rows, 2 * (j + 1) * rows)
-        product = jnp.dot(left[here, :], both, preferred_element_type=jnp.float32)
+        product = products[2 * j * rows : 2 * (j + 1) * rows]
         rc, rs = product[:rows, :TILE], product[:rows, TILE:]
         ic, is_ = product[rows:, :TILE], product[rows:, TILE:]
         buf[slot, 0, j, 0] = rc - is_
@@ -269,6 +269,121 @@
     )(meta, column_sum)
 
 
+def sum_kernel(sizes, x_ref, out_ref, half_in, half_sum, sub_in, sub_sum, row_in, row_sum, pair_in, *sems):
+    n_sub, n_row, n_chunk = sizes
+    sub, row, col = lax.axis_index("sub"), lax.axis_index("frow"), lax.axis_index("fcol")
+    partner = 1 - col
+    barrier = pltpu.get_barrier_semaphore()
+    targets = [{"fcol": partner}]
+    targets += [{"sub": lax.rem(sub + k, n_sub)} for k in range(1, n_sub)]
+    targets += [{"frow": lax.rem(row + k, n_row)} for k in range(1, n_row)]
+    for target in targets:
+        pl.semaphore_signal(barrier, inc=1, device_id=target, device_id_type=pl.DeviceIdType.MESH)
+    pl.semaphore_wait(barrier, len(targets))
+    half_send, half_recv, sub_send, sub_recv, row_send, row_recv, pair_send, pair_recv = sems
+    sub_rows = half_sum.shape[2] // n_sub
+
+    def copy(src, dst, send, recv, target):
+        return pltpu.make_async_remote_copy(
+            src_ref=src, dst_ref=dst, send_sem=send, recv_sem=recv,
+            device_id=target, device_id_type=pl.DeviceIdType.MESH,
+        )
+
+    started = []
+    halves = [
+        copy(x_ref.at[partner * n_chunk + q], half_in.at[q], half_send.at[q], half_recv.at[q], {"fcol": partner})
+        for q in range(n_chunk)
+    ]
+    for one in halves:
+        one.start()
+    started += halves
+    subs = []
+    for q in range(n_chunk):
+        halves[q].wait_recv()
+        half_sum[q] = x_ref[col * n_chunk + q] + half_in[q]
+        mine = []
+        for k in range(1, n_sub):
+            other = lax.rem(sub + k, n_sub)
+            here = pl.ds(pl.multiple_of(other * sub_rows, sub_rows), sub_rows)
+            mine.append(copy(
+                half_sum.at[q, :, here, :], sub_in.at[q, k - 1],
+                sub_send.at[q, k - 1], sub_recv.at[q, k - 1], {"sub": other},
+            ))
+        for one in mine:
+            one.start()
+        subs.append(mine)
+        started += mine
+    rows_sent = []
+    for q in range(n_chunk):
+        own = pl.ds(pl.multiple_of(sub * sub_rows, sub_rows), sub_rows)
+        total = half_sum[q, :, own, :]
+        for k in range(1, n_sub):
+            subs[q][k - 1].wait_recv()
+            total = total + sub_in[q, k - 1]
+        sub_sum[q] = total
+        mine = []
+        for k in range(1, n_row):
+            other = lax.rem(row + k, n_row)
+            here = pl.ds(pl.multiple_of(other * ROW_DEV, ROW_DEV), ROW_DEV)
+            mine.append(copy(
+                sub_sum.at[q, :, here, :], row_in.at[q, k - 1],
+                row_send.at[q, k - 1], row_recv.at[q, k - 1], {"frow": other},
+            ))
+        for one in mine:
+            one.start()
+        rows_sent.append(mine)
+        started += mine
+    pairs = []
+    for q in range(n_chunk):
+        own = pl.ds(pl.multiple_of(row * ROW_DEV, ROW_DEV), ROW_DEV)
+        total = sub_sum[q, :, own, :]
+        for k in range(1, n_row):
+            rows_sent[q][k - 1].wait_recv()
+            total = total + row_in[q, k - 1]
+        row_sum[q] = total
+        out_ref[col * n_chunk + q] = total
+        one = copy(row_sum.at[q], pair_in.at[q], pair_send.at[q], pair_recv.at[q], {"fcol": partner})
+        one.start()
+        pairs.append(one)
+    started += pairs
+    for q in range(n_chunk):
+        pairs[q].wait_recv()
+        out_ref[partner * n_chunk + q] = pair_in[q]
+    for one in started:
+        one.wait_send()
+
+
+def sum_rows(partial_sum):
+    chunks, _, rows, lanes = partial_sum.shape
+    n_sub, n_row = lax.axis_size("sub"), lax.axis_size("frow")
+    q = chunks // 2
+    f32 = jnp.float32
+    dma = pltpu.SemaphoreType.DMA
+    return pl.pallas_call(
+        functools.partial(sum_kernel, (n_sub, n_row, q)),
+        out_shape=jax.ShapeDtypeStruct((chunks, 2, ROW_DEV, lanes), f32),
+        in_specs=[pl.BlockSpec(memory_space=pltpu.VMEM)],
+        out_specs=pl.BlockSpec(memory_space=pltpu.VMEM),
+        scratch_shapes=[
+            pltpu.VMEM((q, 2, rows, lanes), f32),
+            pltpu.VMEM((q, 2, rows, lanes), f32),
+            pltpu.VMEM((q, n_sub - 1, 2, rows // n_sub, lanes), f32),
+            pltpu.VMEM((q, 2, rows // n_sub, lanes), f32),
+            pltpu.VMEM((q, n_row - 1, 2, ROW_DEV, lanes), f32),
+            pltpu.VMEM((q, 2, ROW_DEV, lanes), f32),
+            pltpu.VMEM((q, 2, ROW_DEV, lanes), f32),
+            dma((q,)), dma((q,)),
+            dma((q, n_sub - 1)), dma((q, n_sub - 1)),
+            dma((q, n_row - 1)), dma((q, n_row - 1)),
+            dma((q,)), dma((q,)),
+        ],
+        compiler_params=pltpu.CompilerParams(
+            collective_id=0, has_side_effects=True, vmem_limit_bytes=VMEM_BYTES
+        ),
+        name="sum_rows",
+    )(partial_sum)
+
+
 def local(subgrids, window, counts, nonempty, column_u):
     n_blocks = lax.axis_size("sub") * lax.axis_size("frow")
     rows = ROW_DEV * n_blocks
@@ -276,10 +391,8 @@
     partial_sum = column_partial(
         subgrids, window, counts, nonempty, v_start.astype(jnp.int32).reshape(1), rows
     )
-    own_rows = lax.psum_scatter(
-        partial_sum, ("sub", "frow", "fcol"), scatter_dimension=1, tiled=True
-    )
-    pair_sum = lax.all_gather(own_rows, "fcol", axis=1, tiled=True)
+    chunks = sum_rows(partial_sum)
+    pair_sum = chunks.transpose(1, 2, 0, 3).reshape(2, ROW_DEV, chunks.shape[0] * LANES)
     block = lax.axis_index(("sub", "frow"))
     pair_sum = jnp.where(block < n_blocks // 2, jnp.flip(pair_sum, 1), pair_sum)
     n_local = IMAGE // FACET // lax.axis_size("fcol")

time: 206 us -> 72.2 us (0.35)
  waiting for transfers between devices: 148 us -> 0 us
  Pallas kernels: 39.8 us -> 67.4 us
  between operations: 14.7 us -> 1.32 us
  blocking collectives: 2.24 us -> 0 us
    reduce_scatter x1 -> x0, waiting for transfers between devices: 148 us -> none  [local(): lax.psum_scatter(partial_sum, ('sub', 'frow', 'fcol'), scatter_dimension=...]
    pallas_call x0 -> x1, Pallas kernels: none -> 37.6 us  [sum_rows(): pl.pallas_call(functools.partial(sum_kernel, (n_sub, n_row, q)), out_shap...]
    pallas_call x1, Pallas kernels: 31.9 us -> 21.8 us  [facet_rows(): pl.pallas_call(functools.partial(facet_kernel, n_local), grid=(FACET // 2...]
    all_gather x1 -> x0, blocking collectives: 2.24 us -> none  [local(): pair_sum = lax.all_gather(own_rows, 'fcol', axis=1, tiled=True)]
  transfers between devices with their start and end apart: 1 -> 0, of which waited for: 1 -> 0; matrix products, arithmetic and copies ran while one was open for 0% -> 0% of each run, Pallas kernels for 0% -> 0%
where the time goes in v2:
time: 72.2 us; the launch traced here: 71.9 us
  Pallas kernels  67.4 us (93%)
  other arithmetic  2.21 us (3%)
  between operations  1.32 us (2%)
  local copies, waits for them, and re-layouts  1.03 us (1%)
    pallas_call x1, Pallas kernels, sum_rows(): pl.pallas_call(functools.partial(sum_kernel, (n_sub, n_row, q)), out_shap...  37.6 us
    pallas_call x1, Pallas kernels, facet_rows(): pl.pallas_call(functools.partial(facet_kernel, n_local), grid=(FACET // 2...  21.8 us
    pallas_call x1, Pallas kernels, column_partial(): pl.pallas_call(functools.partial(column_kernel, group), grid=(width // LA...  7.93 us
    select_n x1, other arithmetic, local(): pair_sum = jnp.where(block < n_blocks // 2, jnp.flip(pair_sum, 1), pair_sum)  1.56 us

profile of v2, /device:TPU:0, one launch (start us, length us, event | category | flops | bytes accessed | tf_op | source)
XLA Modules:
  0.0 71.9 jit_solution(9546751596138370060)
XLA Ops:
  1.3 0.6 pad_add_fusion.meta_ref
  1.9 7.9 %column_sum.1.x_ref = f32[4,2,512,128]{3,2,1,0:T(8,128)} custom-call(s32[1]{0:T(128)} %bitcast.1.start_ref, s32[1]{0:T(128)S(6)} %copy.11.count_ref, s32[32]{0:T(128)} %pos_ref.1, f32[32,2,64,512]{3,2,1,0:T(8,128)} %sub_ref.1, f32[64,512]{1,0:T(8,128)} %win_ref.1), custom_call_target="tpu_custom_call" | custom-call | flops 6442450944 | bytes 12582912 | tf_op jit(solution)/shard_map/column_sum/pallas_call | solution.py:117
  9.9 37.6 %sum_rows.1 = f32[4,2,32,128]{3,2,1,0:T(8,128)} custom-call(f32[4,2,512,128]{3,2,1,0:T(8,128)} %column_sum.1.x_ref), custom_call_target="tpu_custom_call" | custom-call | tf_op jit(solution)/shard_map/sum_rows/pallas_call | solution.py:362
  47.5 0.9 %copy_bitcast_fusion = f32[2,32,512]{2,1,0:T(8,128)S(1)} fusion(f32[4,2,32,128]{3,2,1,0:T(8,128)} %sum_rows.1), kind=kLoop, calls=%fused_computation | loop fusion | bytes 262144 | tf_op jit(solution)/shard_map/reshape | solution.py:395
  48.4 0.1 rev.4
  48.5 1.6 %broadcast_select_fusion.sum_ref = f32[2,32,512]{2,1,0:T(8,128)} fusion(f32[2,32,512]{2,1,0:T(8,128)S(1)} %rev.4, pred[]{:T(512)S(6)} %lt.3, f32[4,2,32,128]{3,2,1,0:T(8,128)} %sum_rows.1), kind=kLoop, calls=%fused_computation.1 | loop fusion | flops 32768 | bytes 393217 | tf_op jit(solution)/shard_map/jit(_where)/select_n | solution.py:397
  50.1 21.8 %facet_rows.1 = f32[4,2,32,8192]{3,2,1,0:T(8,128)} custom-call(s32[2]{0:T(128)} %pad_add_fusion.meta_ref, f32[2,32,512]{2,1,0:T(8,128)} %broadcast_select_fusion.sum_ref), custom_call_target="tpu_custom_call" | custom-call | flops 6442450944 | bytes 9437184 | tf_op jit(solution)/shard_map/facet_rows/pallas_call | solution.py:250

commit v3 on v2

--- a/solution.py
+++ b/solution.py
@@ -36,17 +36,26 @@
     return high, low
 
 
-def column_kernel(group, start_ref, count_ref, pos_ref, sub_ref, win_ref, out_ref, left, rot, xs, acc):
+def reverse_rows(x):
+    index = 7 - lax.broadcasted_iota(jnp.int32, (8, LANES), 0)
+    n = x.shape[0] // 8
+    parts = [jnp.take_along_axis(x[(n - 1 - i) * 8 : (n - i) * 8], index, axis=0) for i in range(n)]
+    return jnp.concatenate(parts, 0)
+
+
+def column_kernel(group, count_ref, pos_ref, sub_ref, win_ref, out_ref, left, rot, xs_even, xs_odd, acc):
     cap, _, v_count, _ = sub_ref.shape
     rows = out_ref.shape[2]
     half = rows // 2
     depth = group * v_count
-    n_groups = (count_ref[0] + group - 1) // group
+    n_pairs = (count_ref[0] + 2 * group - 1) // (2 * group)
+    n_groups = 2 * n_pairs
+    v_start = (lax.axis_index("frow") * lax.axis_size("fcol") + lax.axis_index("fcol")) * v_count
 
     @pl.when(pl.program_id(0) == 0)
     def _():
         def one_slot(slot, carry):
-            v = lax.broadcasted_iota(jnp.int32, (v_count, LANES), 0) + start_ref[0]
+            v = lax.broadcasted_iota(jnp.int32, (v_count, LANES), 0) + v_start
             n = v + M * jnp.maximum(pos_ref[slot], 0)
             cos_part, sin_part = sincos((rows - 1) * n)
             live = jnp.where(slot < count_ref[0], 1.0, 0.0)
@@ -65,7 +74,7 @@
             p = jnp.zeros((1, depth), jnp.int32)
             for s in range(group):
                 p = jnp.where(slot_of == s, jnp.maximum(pos_ref[g * group + s], 0), p)
-            n = lane % v_count + start_ref[0] + M * p
+            n = lane % v_count + v_start + M * p
             d = lax.broadcasted_iota(jnp.int32, (step, 1), 0) + r * step
             cos_part, sin_part = sincos((2 * d + 1) * n)
             for part, base in ((cos_part, 0), (sin_part, half)):
@@ -80,7 +89,7 @@
 
     acc[...] = jnp.zeros_like(acc)
 
-    def one_group(g, carry):
+    def build(g, xs):
         for s in range(group):
             slot = g * group + s
             wc = win_ref[...] * rot[slot, 0]
@@ -90,12 +99,22 @@
             high, low = split(x)
             xs[s * v_count : (s + 1) * v_count, :] = high
             xs[depth + s * v_count : depth + (s + 1) * v_count, :] = low
+
+    def multiply(g, xs):
         high = xs[0:depth, :]
         right = jnp.concatenate([high, high, xs[depth : 2 * depth, :]], 0)
         acc[...] += jnp.dot(left[g], right, preferred_element_type=jnp.float32)
+
+    build(0, xs_even)
+
+    def one_pair(i, carry):
+        build(2 * i + 1, xs_odd)
+        multiply(2 * i, xs_even)
+        build(jnp.minimum(2 * i + 2, n_groups - 1), xs_even)
+        multiply(2 * i + 1, xs_odd)
         return carry
 
-    lax.fori_loop(0, n_groups, one_group, 0)
+    lax.fori_loop(0, n_pairs, one_pair, 0)
     n_low = half // ROW_DEV
     for k in range(n_low):
         d = slice(k * ROW_DEV, (k + 1) * ROW_DEV)
@@ -105,13 +124,13 @@
         out_ref[0, 0, e, :] = cr - si
         out_ref[0, 1, e, :] = sr + ci
         lower = slice((n_low - 1 - k) * ROW_DEV, (n_low - k) * ROW_DEV)
-        out_ref[0, 0, lower, :] = cr + si
-        out_ref[0, 1, lower, :] = ci - sr
-
-
-def column_partial(subgrids, window, counts, nonempty, v_start, rows):
+        out_ref[0, 0, lower, :] = reverse_rows(cr + si)
+        out_ref[0, 1, lower, :] = reverse_rows(ci - sr)
+
+
+def column_partial(subgrids, window, counts, nonempty, rows):
     cap, _, v_count, width = subgrids.shape
-    group = min(8, cap)
+    group = min(8, cap // 2)
     depth = group * v_count
     flops = 2 * rows * 2 * width * cap * v_count * 3
     return pl.pallas_call(
@@ -119,7 +138,6 @@
         grid=(width // LANES,),
         out_shape=jax.ShapeDtypeStruct((width // LANES, 2, rows, LANES), jnp.float32),
         in_specs=[
-            pl.BlockSpec(memory_space=pltpu.SMEM),
             pl.BlockSpec(memory_space=pltpu.SMEM),
             pl.BlockSpec(memory_space=pltpu.SMEM),
             pl.BlockSpec((cap, 2, v_count, LANES), lambda t: (0, 0, 0, t)),
@@ -130,12 +148,13 @@
             pltpu.VMEM((cap // group, rows, 3 * depth), jnp.bfloat16),
             pltpu.VMEM((cap, 2, v_count, LANES), jnp.float32),
             pltpu.VMEM((2 * depth, 2 * LANES), jnp.bfloat16),
+            pltpu.VMEM((2 * depth, 2 * LANES), jnp.bfloat16),
             pltpu.VMEM((rows, 2 * LANES), jnp.float32),
         ],
         compiler_params=pltpu.CompilerParams(vmem_limit_bytes=VMEM_BYTES),
         cost_estimate=pl.CostEstimate(flops=flops, bytes_accessed=12 << 20, transcendentals=0),
         name="column_sum",
-    )(v_start, counts, nonempty, subgrids, window)
+    )(counts, nonempty, subgrids, window)
 
 
 TILE = 512
@@ -151,12 +170,13 @@
     return jnp.concatenate(parts, 1)
 
 
-def facet_kernel(n_local, meta_ref, sum_ref, out_ref, left, base, right, buf, sem):
+def facet_kernel(n_local, column_ref, sum_ref, out_ref, left, base, turn, right, buf, sem):
     t = pl.program_id(0)
     steps = pl.num_programs(0)
-    column = meta_ref[0]
-    first = meta_ref[1]
-    rows = sum_ref.shape[1]
+    column = column_ref[0]
+    first = lax.axis_index("fcol") * n_local
+    rows = sum_ref.shape[2]
+    chunks = sum_ref.shape[0]
     mid = FACET // 2
 
     @pl.when(t == 0)
@@ -165,7 +185,8 @@
         w = (u + column) & (IMAGE - 1)
         for j in range(n_local):
             cos_part, sin_part = sincos((2 * FACET * (first + j) + FACET - 1) * w)
-            re, im = sum_ref[0], sum_ref[1]
+            re = jnp.concatenate([sum_ref[q, 0] for q in range(chunks)], 1)
+            im = jnp.concatenate([sum_ref[q, 1] for q in range(chunks)], 1)
             for part, value in ((0, re * cos_part - im * sin_part), (1, re * sin_part + im * cos_part)):
                 high, low = split(value)
                 here = slice((2 * j + part) * rows, (2 * j + part + 1) * rows)
@@ -184,24 +205,13 @@
 
         lax.fori_loop(0, M // 16, one_block, 0)
 
-    def one_block(i, carry):
+    def one_turn(i, carry):
         here = pl.ds(pl.multiple_of(i * 16, 16), 16)
-        low_here = pl.ds(pl.multiple_of(M + i * 16, 16), 16)
         w = (lax.broadcasted_iota(jnp.int32, (16, LANES), 0) + i * 16 + column) & (IMAGE - 1)
-        tc, ts = sincos((2 * TILE * t) * w)
-        for k in range(TILE // LANES):
-            lanes = slice(k * LANES, (k + 1) * LANES)
-            bc, bs = base[0, here, lanes], base[1, here, lanes]
-            high, low = split(bc * tc - bs * ts)
-            right[here, lanes] = high
-            right[low_here, lanes] = low
-            lanes = slice(TILE + k * LANES, TILE + (k + 1) * LANES)
-            high, low = split(bc * ts + bs * tc)
-            right[here, lanes] = high
-            right[low_here, lanes] = low
+        turn[0, here, :], turn[1, here, :] = sincos((2 * TILE * t) * w)
         return carry
 
-    lax.fori_loop(0, M // 16, one_block, 0, unroll=2)
+    lax.fori_loop(0, M // 16, one_turn, 0, unroll=4)
     slot = lax.rem(t, 2)
 
     def copies(step, place):
@@ -222,17 +232,36 @@
         for copy in copies(t - 2, slot):
             copy.wait()
 
-    high = right[0:M, :]
-    both = jnp.concatenate([high, high, right[M : 2 * M, :]], 0)
-    products = jnp.dot(left[...], both, preferred_element_type=jnp.float32)
-    for j in range(n_local):
-        product = products[2 * j * rows : 2 * (j + 1) * rows]
-        rc, rs = product[:rows, :TILE], product[:rows, TILE:]
-        ic, is_ = product[rows:, :TILE], product[rows:, TILE:]
-        buf[slot, 0, j, 0] = rc - is_
-        buf[slot, 0, j, 1] = rs + ic
-        buf[slot, 1, j, 0] = reverse_lanes(rc + is_)
-        buf[slot, 1, j, 1] = reverse_lanes(ic - rs)
+    def build(k):
+        lanes = slice(k * LANES, (k + 1) * LANES)
+        for i in range(M // 16):
+            here = slice(i * 16, (i + 1) * 16)
+            bc, bs = base[0, here, lanes], base[1, here, lanes]
+            tc, ts = turn[0, here, :], turn[1, here, :]
+            for part, value in ((0, bc * tc - bs * ts), (1, bc * ts + bs * tc)):
+                high, low = split(value)
+                place = slice(part * LANES, (part + 1) * LANES)
+                right[k, here, place] = high
+                right[k, M + i * 16 : M + (i + 1) * 16, place] = low
+
+    n_tiles = TILE // LANES
+    build(0)
+    for k in range(n_tiles):
+        if k + 1 < n_tiles:
+            build(k + 1)
+        high = right[k, 0:M, :]
+        both = jnp.concatenate([high, high, right[k, M : 2 * M, :]], 0)
+        products = jnp.dot(left[...], both, preferred_element_type=jnp.float32)
+        upper = slice(k * LANES, (k + 1) * LANES)
+        lower = slice((n_tiles - 1 - k) * LANES, (n_tiles - k) * LANES)
+        for j in range(n_local):
+            product = products[2 * j * rows : 2 * (j + 1) * rows]
+            rc, rs = product[:rows, :LANES], product[:rows, LANES:]
+            ic, is_ = product[rows:, :LANES], product[rows:, LANES:]
+            buf[slot, 0, j, 0, :, upper] = rc - is_
+            buf[slot, 0, j, 1, :, upper] = rs + ic
+            buf[slot, 1, j, 0, :, lower] = reverse_lanes(rc + is_)
+            buf[slot, 1, j, 1, :, lower] = reverse_lanes(ic - rs)
     for copy in copies(t, slot):
         copy.start()
 
@@ -244,8 +273,8 @@
             copy.wait()
 
 
-def facet_rows(column_sum, meta, n_local):
-    rows = column_sum.shape[1]
+def facet_rows(column_sum, column_u, n_local):
+    rows = column_sum.shape[2]
     flops = 2 * (2 * n_local * rows) * (3 * M) * FACET
     return pl.pallas_call(
         functools.partial(facet_kernel, n_local),
@@ -253,20 +282,21 @@
         out_shape=jax.ShapeDtypeStruct((n_local, 2, rows, FACET), jnp.float32),
         in_specs=[
             pl.BlockSpec(memory_space=pltpu.SMEM),
-            pl.BlockSpec((2, rows, M), lambda t: (0, 0, 0)),
+            pl.BlockSpec(column_sum.shape, lambda t: (0, 0, 0, 0)),
         ],
         out_specs=pl.BlockSpec(memory_space=pl.ANY),
         scratch_shapes=[
             pltpu.VMEM((2 * n_local * rows, 3 * M), jnp.bfloat16),
             pltpu.VMEM((2, M, TILE), jnp.float32),
-            pltpu.VMEM((2 * M, 2 * TILE), jnp.bfloat16),
+            pltpu.VMEM((2, M, LANES), jnp.float32),
+            pltpu.VMEM((TILE // LANES, 2 * M, 2 * LANES), jnp.bfloat16),
             pltpu.VMEM((2, 2, n_local, 2, rows, TILE), jnp.float32),
             pltpu.SemaphoreType.DMA((2, 2)),
         ],
         compiler_params=pltpu.CompilerParams(vmem_limit_bytes=VMEM_BYTES),
         cost_estimate=pl.CostEstimate(flops=flops, bytes_accessed=9 << 20, transcendentals=0),
         name="facet_rows",
-    )(meta, column_sum)
+    )(column_u, column_sum)
 
 
 def sum_kernel(sizes, x_ref, out_ref, half_in, half_sum, sub_in, sub_sum, row_in, row_sum, pair_in, *sems):
@@ -387,17 +417,9 @@
 def local(subgrids, window, counts, nonempty, column_u):
     n_blocks = lax.axis_size("sub") * lax.axis_size("frow")
     rows = ROW_DEV * n_blocks
-    v_start = lax.axis_index(("frow", "fcol")) * subgrids.shape[2]
-    partial_sum = column_partial(
-        subgrids, window, counts, nonempty, v_start.astype(jnp.int32).reshape(1), rows
-    )
-    chunks = sum_rows(partial_sum)
-    pair_sum = chunks.transpose(1, 2, 0, 3).reshape(2, ROW_DEV, chunks.shape[0] * LANES)
-    block = lax.axis_index(("sub", "frow"))
-    pair_sum = jnp.where(block < n_blocks // 2, jnp.flip(pair_sum, 1), pair_sum)
+    partial_sum = column_partial(subgrids, window, counts, nonempty, rows)
     n_local = IMAGE // FACET // lax.axis_size("fcol")
-    meta = jnp.stack([column_u[0], (lax.axis_index("fcol") * n_local).astype(jnp.int32)])
-    return facet_rows(pair_sum, meta, n_local)
+    return facet_rows(sum_rows(partial_sum), column_u, n_local)
 
 
 def solution(mesh):

time: 72.2 us -> 62.2 us (0.86)
  Pallas kernels: 67.4 us -> 60.6 us
  other arithmetic: 2.21 us -> 0 us
  local copies, waits for them, and re-layouts: 1.03 us -> 0 us
    pallas_call x1, Pallas kernels: 21.8 us -> 16.4 us  [facet_rows(): pl.pallas_call(functools.partial(facet_kernel, n_local), grid=(FACET // 2...]
    pallas_call x1, Pallas kernels: 37.6 us -> 33.5 us  [sum_rows(): pl.pallas_call(functools.partial(sum_kernel, (n_sub, n_row, q)), out_shap...]
    pallas_call x1, Pallas kernels: 7.93 us -> 10.8 us  [column_partial(): pl.pallas_call(functools.partial(column_kernel, group), grid=(width // LA...]
    select_n x1 -> x0, other arithmetic: 1.56 us -> none  [local(): pair_sum = jnp.where(block < n_blocks // 2, jnp.flip(pair_sum, 1), pair_sum)]
    reshape x1 -> x0, local copies, waits for them, and re-layouts: 0.91 us -> none  [local(): chunks.transpose(1, 2, 0, 3).reshape(2, ROW_DEV, chunks.shape[0] * LANES)]
where the time goes in v3:
time: 62.2 us; the launch traced here: 61.9 us
  Pallas kernels  60.6 us (97%)
  between operations  1.31 us (2%)
    pallas_call x1, Pallas kernels, sum_rows(): pl.pallas_call(functools.partial(sum_kernel, (n_sub, n_row, q)), out_shap...  33.5 us
    pallas_call x1, Pallas kernels, facet_rows(): pl.pallas_call(functools.partial(facet_kernel, n_local), grid=(FACET // 2...  16.4 us
    pallas_call x1, Pallas kernels, column_partial(): pl.pallas_call(functools.partial(column_kernel, group), grid=(width // LA...  10.8 us

profile of v3, /device:TPU:0, one launch (start us, length us, event | category | flops | bytes accessed | tf_op | source)
XLA Modules:
  0.0 61.9 jit_solution(6259560897676096913)
XLA Ops:
  1.3 10.8 %column_sum.1.x_ref = f32[4,2,512,128]{3,2,1,0:T(8,128)} custom-call(s32[1]{0:T(128)S(6)} %copy.6.count_ref, s32[32]{0:T(128)} %pos_ref.1, f32[32,2,64,512]{3,2,1,0:T(8,128)} %sub_ref.1, f32[64,512]{1,0:T(8,128)} %win_ref.1), custom_call_target="tpu_custom_call" | custom-call | flops 6442450944 | bytes 12582912 | tf_op jit(solution)/shard_map/column_sum/pallas_call | solution.py:136
  12.1 33.5 %sum_rows.1.sum_ref = f32[4,2,32,128]{3,2,1,0:T(8,128)} custom-call(f32[4,2,512,128]{3,2,1,0:T(8,128)} %column_sum.1.x_ref), custom_call_target="tpu_custom_call" | custom-call | tf_op jit(solution)/shard_map/sum_rows/pallas_call | solution.py:392
  45.6 16.4 %facet_rows.1 = f32[4,2,32,8192]{3,2,1,0:T(8,128)} custom-call(s32[1]{0:T(128)S(6)} %copy.7.column_ref, f32[4,2,32,128]{3,2,1,0:T(8,128)} %sum_rows.1.sum_ref), custom_call_target="tpu_custom_call" | custom-call | flops 6442450944 | bytes 9437184 | tf_op jit(solution)/shard_map/facet_rows/pallas_call | solution.py:279

commit v4 on v3

--- a/solution.py
+++ b/solution.py
@@ -170,7 +170,7 @@
     return jnp.concatenate(parts, 1)
 
 
-def facet_kernel(n_local, column_ref, sum_ref, out_ref, left, base, turn, right, buf, sem):
+def facet_kernel(n_local, column_ref, sum_ref, right, out_ref, left, buf, sem):
     t = pl.program_id(0)
     steps = pl.num_programs(0)
     column = column_ref[0]
@@ -194,24 +194,6 @@
                 left[here, M : 2 * M] = low
                 left[here, 2 * M : 3 * M] = high
 
-        def one_block(i, carry):
-            here = pl.ds(pl.multiple_of(i * 16, 16), 16)
-            w = (lax.broadcasted_iota(jnp.int32, (16, 1), 0) + i * 16 + column) & (IMAGE - 1)
-            d = lax.broadcasted_iota(jnp.int32, (1, TILE), 1)
-            cos_part, sin_part = sincos((2 * d + 1) * w)
-            base[0, here, :] = cos_part
-            base[1, here, :] = sin_part
-            return carry
-
-        lax.fori_loop(0, M // 16, one_block, 0)
-
-    def one_turn(i, carry):
-        here = pl.ds(pl.multiple_of(i * 16, 16), 16)
-        w = (lax.broadcasted_iota(jnp.int32, (16, LANES), 0) + i * 16 + column) & (IMAGE - 1)
-        turn[0, here, :], turn[1, here, :] = sincos((2 * TILE * t) * w)
-        return carry
-
-    lax.fori_loop(0, M // 16, one_turn, 0, unroll=4)
     slot = lax.rem(t, 2)
 
     def copies(step, place):
@@ -232,23 +214,8 @@
         for copy in copies(t - 2, slot):
             copy.wait()
 
-    def build(k):
-        lanes = slice(k * LANES, (k + 1) * LANES)
-        for i in range(M // 16):
-            here = slice(i * 16, (i + 1) * 16)
-            bc, bs = base[0, here, lanes], base[1, here, lanes]
-            tc, ts = turn[0, here, :], turn[1, here, :]
-            for part, value in ((0, bc * tc - bs * ts), (1, bc * ts + bs * tc)):
-                high, low = split(value)
-                place = slice(part * LANES, (part + 1) * LANES)
-                right[k, here, place] = high
-                right[k, M + i * 16 : M + (i + 1) * 16, place] = low
-
     n_tiles = TILE // LANES
-    build(0)
     for k in range(n_tiles):
-        if k + 1 < n_tiles:
-            build(k + 1)
         high = right[k, 0:M, :]
         both = jnp.concatenate([high, high, right[k, M : 2 * M, :]], 0)
         products = jnp.dot(left[...], both, preferred_element_type=jnp.float32)
@@ -273,7 +240,7 @@
             copy.wait()
 
 
-def facet_rows(column_sum, column_u, n_local):
+def facet_rows(column_sum, table, column_u, n_local):
     rows = column_sum.shape[2]
     flops = 2 * (2 * n_local * rows) * (3 * M) * FACET
     return pl.pallas_call(
@@ -283,23 +250,21 @@
         in_specs=[
             pl.BlockSpec(memory_space=pltpu.SMEM),
             pl.BlockSpec(column_sum.shape, lambda t: (0, 0, 0, 0)),
+            pl.BlockSpec((TILE // LANES, 2 * M, 2 * LANES), lambda t: (t, 0, 0)),
         ],
         out_specs=pl.BlockSpec(memory_space=pl.ANY),
         scratch_shapes=[
             pltpu.VMEM((2 * n_local * rows, 3 * M), jnp.bfloat16),
-            pltpu.VMEM((2, M, TILE), jnp.float32),
-            pltpu.VMEM((2, M, LANES), jnp.float32),
-            pltpu.VMEM((TILE // LANES, 2 * M, 2 * LANES), jnp.bfloat16),
             pltpu.VMEM((2, 2, n_local, 2, rows, TILE), jnp.float32),
             pltpu.SemaphoreType.DMA((2, 2)),
         ],
         compiler_params=pltpu.CompilerParams(vmem_limit_bytes=VMEM_BYTES),
-        cost_estimate=pl.CostEstimate(flops=flops, bytes_accessed=9 << 20, transcendentals=0),
+        cost_estimate=pl.CostEstimate(flops=flops, bytes_accessed=25 << 20, transcendentals=0),
         name="facet_rows",
-    )(column_u, column_sum)
-
-
-def sum_kernel(sizes, x_ref, out_ref, half_in, half_sum, sub_in, sub_sum, row_in, row_sum, pair_in, *sems):
+    )(column_u, column_sum, table)
+
+
+def sum_kernel(sizes, column_ref, x_ref, out_ref, table_ref, base, turn, table, table_sem, half_in, half_sum, sub_in, sub_sum, row_in, row_sum, pair_in, *sems):
     n_sub, n_row, n_chunk = sizes
     sub, row, col = lax.axis_index("sub"), lax.axis_index("frow"), lax.axis_index("fcol")
     partner = 1 - col
@@ -327,6 +292,41 @@
     for one in halves:
         one.start()
     started += halves
+    n_tiles = TILE // LANES
+    n_steps = FACET // 2 // TILE
+
+    def first_tile(i, carry):
+        here = pl.ds(pl.multiple_of(i * 16, 16), 16)
+        w = (lax.broadcasted_iota(jnp.int32, (16, LANES), 0) + i * 16 + column_ref[0]) & (IMAGE - 1)
+        d = lax.broadcasted_iota(jnp.int32, (16, LANES), 1)
+        base[0, here, :], base[1, here, :] = sincos((2 * d + 1) * w)
+        turn[0, here, :], turn[1, here, :] = sincos(2 * LANES * w)
+        return carry
+
+    lax.fori_loop(0, M // 16, first_tile, 0)
+
+    def build(step):
+        def one_block(i, carry):
+            here = pl.ds(pl.multiple_of(i * 16, 16), 16)
+            low_here = pl.ds(pl.multiple_of(M + i * 16, 16), 16)
+            c, s = base[0, here, :], base[1, here, :]
+            tc, ts = turn[0, here, :], turn[1, here, :]
+            for k in range(n_tiles):
+                for part, value in ((0, c), (1, s)):
+                    high, low = split(value)
+                    place = slice(part * LANES, (part + 1) * LANES)
+                    table[step * n_tiles + k, here, place] = high
+                    table[step * n_tiles + k, low_here, place] = low
+                c, s = c * tc - s * ts, c * ts + s * tc
+            base[0, here, :], base[1, here, :] = c, s
+            return carry
+
+        lax.fori_loop(0, M // 16, one_block, 0)
+        tiles = slice(step * n_tiles, (step + 1) * n_tiles)
+        one = pltpu.make_async_copy(table.at[tiles], table_ref.at[tiles], table_sem.at[step])
+        one.start()
+        return one
+
     subs = []
     for q in range(n_chunk):
         halves[q].wait_recv()
@@ -343,6 +343,7 @@
             one.start()
         subs.append(mine)
         started += mine
+    built = [build(step) for step in range(n_steps // 2)]
     rows_sent = []
     for q in range(n_chunk):
         own = pl.ds(pl.multiple_of(sub * sub_rows, sub_rows), sub_rows)
@@ -363,6 +364,9 @@
             one.start()
         rows_sent.append(mine)
         started += mine
+        if q == 0:
+            built += [build(step) for step in range(n_steps // 2, n_steps - 1)]
+    built.append(build(n_steps - 1))
     pairs = []
     for q in range(n_chunk):
         own = pl.ds(pl.multiple_of(row * ROW_DEV, ROW_DEV), ROW_DEV)
@@ -381,9 +385,11 @@
         out_ref[partner * n_chunk + q] = pair_in[q]
     for one in started:
         one.wait_send()
-
-
-def sum_rows(partial_sum):
+    for one in built:
+        one.wait()
+
+
+def sum_rows(partial_sum, column_u):
     chunks, _, rows, lanes = partial_sum.shape
     n_sub, n_row = lax.axis_size("sub"), lax.axis_size("frow")
     q = chunks // 2
@@ -391,10 +397,20 @@
     dma = pltpu.SemaphoreType.DMA
     return pl.pallas_call(
         functools.partial(sum_kernel, (n_sub, n_row, q)),
-        out_shape=jax.ShapeDtypeStruct((chunks, 2, ROW_DEV, lanes), f32),
-        in_specs=[pl.BlockSpec(memory_space=pltpu.VMEM)],
-        out_specs=pl.BlockSpec(memory_space=pltpu.VMEM),
+        out_shape=(
+            jax.ShapeDtypeStruct((chunks, 2, ROW_DEV, lanes), f32),
+            jax.ShapeDtypeStruct((FACET // 2 // LANES, 2 * M, 2 * LANES), jnp.bfloat16),
+        ),
+        in_specs=[
+            pl.BlockSpec(memory_space=pltpu.SMEM),
+            pl.BlockSpec(memory_space=pltpu.VMEM),
+        ],
+        out_specs=(pl.BlockSpec(memory_space=pltpu.VMEM), pl.BlockSpec(memory_space=pl.ANY)),
         scratch_shapes=[
+            pltpu.VMEM((2, M, LANES), f32),
+            pltpu.VMEM((2, M, LANES), f32),
+            pltpu.VMEM((FACET // 2 // LANES, 2 * M, 2 * LANES), jnp.bfloat16),
+            dma((FACET // 2 // TILE,)),
             pltpu.VMEM((q, 2, rows, lanes), f32),
             pltpu.VMEM((q, 2, rows, lanes), f32),
             pltpu.VMEM((q, n_sub - 1, 2, rows // n_sub, lanes), f32),
@@ -411,7 +427,7 @@
             collective_id=0, has_side_effects=True, vmem_limit_bytes=VMEM_BYTES
         ),
         name="sum_rows",
-    )(partial_sum)
+    )(column_u, partial_sum)
 
 
 def local(subgrids, window, counts, nonempty, column_u):
@@ -419,7 +435,8 @@
     rows = ROW_DEV * n_blocks
     partial_sum = column_partial(subgrids, window, counts, nonempty, rows)
     n_local = IMAGE // FACET // lax.axis_size("fcol")
-    return facet_rows(sum_rows(partial_sum), column_u, n_local)
+    column_sum, table = sum_rows(partial_sum, column_u)
+    return facet_rows(column_sum, table, column_u, n_local)
 
 
 def solution(mesh):

time: 62.2 us -> 60.7 us (0.976)
  Pallas kernels: 60.6 us -> 59 us
    pallas_call x1, Pallas kernels: 16.4 us -> 14.6 us  [facet_rows(): pl.pallas_call(functools.partial(facet_kernel, n_local), grid=(FACET // 2...]
where the time goes in v4:
time: 60.7 us; the launch traced here: 60.3 us
  Pallas kernels  59 us (97%)
  between operations  1.31 us (2%)
    pallas_call x1, Pallas kernels, sum_rows(): pl.pallas_call(functools.partial(sum_kernel, (n_sub, n_row, q)), out_shap...  33.7 us
    pallas_call x1, Pallas kernels, facet_rows(): pl.pallas_call(functools.partial(facet_kernel, n_local), grid=(FACET // 2...  14.6 us
    pallas_call x1, Pallas kernels, column_partial(): pl.pallas_call(functools.partial(column_kernel, group), grid=(width // LA...  10.8 us

profile of v4, /device:TPU:0, one launch (start us, length us, event | category | flops | bytes accessed | tf_op | source)
XLA Modules:
  0.0 60.3 jit_solution(15512235855547087461)
XLA Ops:
  1.3 10.8 %column_sum.1.x_ref = f32[4,2,512,128]{3,2,1,0:T(8,128)} custom-call(s32[1]{0:T(128)S(6)} %copy.6.count_ref, s32[32]{0:T(128)} %pos_ref.1, f32[32,2,64,512]{3,2,1,0:T(8,128)} %sub_ref.1, f32[64,512]{1,0:T(8,128)} %win_ref.1), custom_call_target="tpu_custom_call" | custom-call | flops 6442450944 | bytes 12582912 | tf_op jit(solution)/shard_map/column_sum/pallas_call | solution.py:136
  12.1 33.7 %sum_rows.1 = (f32[4,2,32,128]{3,2,1,0:T(8,128)}, bf16[32,1024,256]{2,1,0:T(8,128)(2,1)}) custom-call(s32[1]{0:T(128)S(6)} %copy.7.column_ref, f32[4,2,512,128]{3,2,1,0:T(8,128)} %column_sum.1.x_ref), custom_call_target="tpu_custom_call" | custom-call | tf_op jit(solution)/shard_map/sum_rows/pallas_call | solution.py:398
  45.8 14.6 %facet_rows.1 = f32[4,2,32,8192]{3,2,1,0:T(8,128)} custom-call(s32[1]{0:T(128)S(6)} %copy.7.column_ref, f32[4,2,32,128]{3,2,1,0:T(8,128)} %get-tuple-element.7.sum_ref, bf16[32,1024,256]{2,1,0:T(8,128)(2,1)} %get-tuple-element.8.right), custom_call_target="tpu_custom_call" | custom-call | flops 6442450944 | bytes 26214400 | tf_op jit(solution)/shard_map/facet_rows/pallas_call | solution.py:246

commit v5 on v4

--- a/solution.py
+++ b/solution.py
@@ -178,6 +178,7 @@
     rows = sum_ref.shape[2]
     chunks = sum_ref.shape[0]
     mid = FACET // 2
+    n_left = 2 * n_local * rows
 
     @pl.when(t == 0)
     def _():
@@ -190,9 +191,8 @@
             for part, value in ((0, re * cos_part - im * sin_part), (1, re * sin_part + im * cos_part)):
                 high, low = split(value)
                 here = slice((2 * j + part) * rows, (2 * j + part + 1) * rows)
-                left[here, 0:M] = high
-                left[here, M : 2 * M] = low
-                left[here, 2 * M : 3 * M] = high
+                left[here, :] = high
+                left[slice(here.start + n_left, here.stop + n_left), :] = low
 
     slot = lax.rem(t, 2)
 
@@ -217,8 +217,10 @@
     n_tiles = TILE // LANES
     for k in range(n_tiles):
         high = right[k, 0:M, :]
-        both = jnp.concatenate([high, high, right[k, M : 2 * M, :]], 0)
-        products = jnp.dot(left[...], both, preferred_element_type=jnp.float32)
+        low = right[k, M : 2 * M, :]
+        stacked = jnp.dot(left[...], high, preferred_element_type=jnp.float32)
+        products = jnp.dot(left[0:n_left, :], low, preferred_element_type=jnp.float32)
+        products = products + stacked[:n_left] + stacked[n_left:]
         upper = slice(k * LANES, (k + 1) * LANES)
         lower = slice((n_tiles - 1 - k) * LANES, (n_tiles - k) * LANES)
         for j in range(n_local):
@@ -254,7 +256,7 @@
         ],
         out_specs=pl.BlockSpec(memory_space=pl.ANY),
         scratch_shapes=[
-            pltpu.VMEM((2 * n_local * rows, 3 * M), jnp.bfloat16),
+            pltpu.VMEM((4 * n_local * rows, M), jnp.bfloat16),
             pltpu.VMEM((2, 2, n_local, 2, rows, TILE), jnp.float32),
             pltpu.SemaphoreType.DMA((2, 2)),
         ],
@@ -343,7 +345,7 @@
             one.start()
         subs.append(mine)
         started += mine
-    built = [build(step) for step in range(n_steps // 2)]
+    built = [build(step) for step in range(3)]
     rows_sent = []
     for q in range(n_chunk):
         own = pl.ds(pl.multiple_of(sub * sub_rows, sub_rows), sub_rows)
@@ -364,9 +366,9 @@
             one.start()
         rows_sent.append(mine)
         started += mine
-        if q == 0:
-            built += [build(step) for step in range(n_steps // 2, n_steps - 1)]
-    built.append(build(n_steps - 1))
+        if q < n_chunk - 1:
+            built.append(build(3 + q))
+    built += [build(step) for step in range(2 + n_chunk, n_steps)]
     pairs = []
     for q in range(n_chunk):
         own = pl.ds(pl.multiple_of(row * ROW_DEV, ROW_DEV), ROW_DEV)
@@ -390,7 +392,9 @@
 
 
 def sum_rows(partial_sum, column_u):
-    chunks, _, rows, lanes = partial_sum.shape
+    rows, lanes = partial_sum.shape[2:]
+    partial_sum = partial_sum.reshape(-1, 1, rows, lanes)
+    chunks = partial_sum.shape[0]
     n_sub, n_row = lax.axis_size("sub"), lax.axis_size("frow")
     q = chunks // 2
     f32 = jnp.float32
@@ -398,7 +402,7 @@
     return pl.pallas_call(
         functools.partial(sum_kernel, (n_sub, n_row, q)),
         out_shape=(
-            jax.ShapeDtypeStruct((chunks, 2, ROW_DEV, lanes), f32),
+            jax.ShapeDtypeStruct((chunks, 1, ROW_DEV, lanes), f32),
             jax.ShapeDtypeStruct((FACET // 2 // LANES, 2 * M, 2 * LANES), jnp.bfloat16),
         ),
         in_specs=[
@@ -411,13 +415,13 @@
             pltpu.VMEM((2, M, LANES), f32),
             pltpu.VMEM((FACET // 2 // LANES, 2 * M, 2 * LANES), jnp.bfloat16),
             dma((FACET // 2 // TILE,)),
-            pltpu.VMEM((q, 2, rows, lanes), f32),
-            pltpu.VMEM((q, 2, rows, lanes), f32),
-            pltpu.VMEM((q, n_sub - 1, 2, rows // n_sub, lanes), f32),
-            pltpu.VMEM((q, 2, rows // n_sub, lanes), f32),
-            pltpu.VMEM((q, n_row - 1, 2, ROW_DEV, lanes), f32),
-            pltpu.VMEM((q, 2, ROW_DEV, lanes), f32),
-            pltpu.VMEM((q, 2, ROW_DEV, lanes), f32),
+            pltpu.VMEM((q, 1, rows, lanes), f32),
+            pltpu.VMEM((q, 1, rows, lanes), f32),
+            pltpu.VMEM((q, n_sub - 1, 1, rows // n_sub, lanes), f32),
+            pltpu.VMEM((q, 1, rows // n_sub, lanes), f32),
+            pltpu.VMEM((q, n_row - 1, 1, ROW_DEV, lanes), f32),
+            pltpu.VMEM((q, 1, ROW_DEV, lanes), f32),
+            pltpu.VMEM((q, 1, ROW_DEV, lanes), f32),
             dma((q,)), dma((q,)),
             dma((q, n_sub - 1)), dma((q, n_sub - 1)),
             dma((q, n_row - 1)), dma((q, n_row - 1)),
@@ -436,6 +440,7 @@
     partial_sum = column_partial(subgrids, window, counts, nonempty, rows)
     n_local = IMAGE // FACET // lax.axis_size("fcol")
     column_sum, table = sum_rows(partial_sum, column_u)
+    column_sum = column_sum.reshape(-1, 2, ROW_DEV, LANES)
     return facet_rows(column_sum, table, column_u, n_local)
 
 

time: 60.7 us -> 60.1 us (level)
  no operation moved by 1% of the time
where the time goes in v5:
time: 60.1 us; the launch traced here: 60.2 us
  Pallas kernels  58.9 us (98%)
  between operations  1.31 us (2%)
    pallas_call x1, Pallas kernels, sum_rows(): pl.pallas_call(functools.partial(sum_kernel, (n_sub, n_row, q)), out_shap...  33.5 us
    pallas_call x1, Pallas kernels, facet_rows(): pl.pallas_call(functools.partial(facet_kernel, n_local), grid=(FACET // 2...  14.5 us
    pallas_call x1, Pallas kernels, column_partial(): pl.pallas_call(functools.partial(column_kernel, group), grid=(width // LA...  10.8 us

profile of v5, /device:TPU:0, one launch (start us, length us, event | category | flops | bytes accessed | tf_op | source)
XLA Modules:
  0.0 60.2 jit_solution(1868609666724619757)
XLA Ops:
  1.3 10.8 %column_sum.1 = f32[4,2,512,128]{3,2,1,0:T(8,128)} custom-call(s32[1]{0:T(128)S(6)} %copy.6.count_ref, s32[32]{0:T(128)} %pos_ref.1, f32[32,2,64,512]{3,2,1,0:T(8,128)} %sub_ref.1, f32[64,512]{1,0:T(8,128)} %win_ref.1), custom_call_target="tpu_custom_call" | custom-call | flops 6442450944 | bytes 12582912 | tf_op jit(solution)/shard_map/column_sum/pallas_call | solution.py:136
  12.1 33.5 %sum_rows.1 = (f32[8,1,32,128]{3,2,1,0:T(8,128)}, bf16[32,1024,256]{2,1,0:T(8,128)(2,1)}) custom-call(s32[1]{0:T(128)S(6)} %copy.7.column_ref, f32[8,1,512,128]{3,2,1,0:T(8,128)} %bitcast.2), custom_call_target="tpu_custom_call" | custom-call | tf_op jit(solution)/shard_map/sum_rows/pallas_call | solution.py:402
  45.6 14.5 %facet_rows.1 = f32[4,2,32,8192]{3,2,1,0:T(8,128)} custom-call(s32[1]{0:T(128)S(6)} %copy.7.column_ref, f32[4,2,32,128]{3,2,1,0:T(8,128)} %bitcast.3, bf16[32,1024,256]{2,1,0:T(8,128)(2,1)} %get-tuple-element.8.right), custom_call_target="tpu_custom_call" | custom-call | flops 6442450944 | bytes 26214400 | tf_op jit(solution)/shard_map/facet_rows/pallas_call | solution.py:248

commit v6 on v5

--- a/solution.py
+++ b/solution.py
@@ -305,7 +305,7 @@
         turn[0, here, :], turn[1, here, :] = sincos(2 * LANES * w)
         return carry
 
-    lax.fori_loop(0, M // 16, first_tile, 0)
+    lax.fori_loop(0, M // 16, first_tile, 0, unroll=2)
 
     def build(step):
         def one_block(i, carry):
@@ -323,7 +323,7 @@
             base[0, here, :], base[1, here, :] = c, s
             return carry
 
-        lax.fori_loop(0, M // 16, one_block, 0)
+        lax.fori_loop(0, M // 16, one_block, 0, unroll=2)
         tiles = slice(step * n_tiles, (step + 1) * n_tiles)
         one = pltpu.make_async_copy(table.at[tiles], table_ref.at[tiles], table_sem.at[step])
         one.start()

time: 60.1 us -> 60.4 us (level)
  no operation moved by 1% of the time
where the time goes in v6:
time: 60.4 us; the launch traced here: 60 us
  Pallas kernels  58.7 us (97%)
  between operations  1.31 us (2%)
    pallas_call x1, Pallas kernels, sum_rows(): pl.pallas_call(functools.partial(sum_kernel, (n_sub, n_row, q)), out_shap...  33.4 us
    pallas_call x1, Pallas kernels, facet_rows(): pl.pallas_call(functools.partial(facet_kernel, n_local), grid=(FACET // 2...  14.5 us
    pallas_call x1, Pallas kernels, column_partial(): pl.pallas_call(functools.partial(column_kernel, group), grid=(width // LA...  10.8 us

profile of v6, /device:TPU:0, one launch (start us, length us, event | category | flops | bytes accessed | tf_op | source)
XLA Modules:
  0.0 60.0 jit_solution(6408704668103920478)
XLA Ops:
  1.3 10.8 %column_sum.1 = f32[4,2,512,128]{3,2,1,0:T(8,128)} custom-call(s32[1]{0:T(128)S(6)} %copy.6.count_ref, s32[32]{0:T(128)} %pos_ref.1, f32[32,2,64,512]{3,2,1,0:T(8,128)} %sub_ref.1, f32[64,512]{1,0:T(8,128)} %win_ref.1), custom_call_target="tpu_custom_call" | custom-call | flops 6442450944 | bytes 12582912 | tf_op jit(solution)/shard_map/column_sum/pallas_call | solution.py:136
  12.1 33.4 %sum_rows.1 = (f32[8,1,32,128]{3,2,1,0:T(8,128)}, bf16[32,1024,256]{2,1,0:T(8,128)(2,1)}) custom-call(s32[1]{0:T(128)S(6)} %copy.7.column_ref, f32[8,1,512,128]{3,2,1,0:T(8,128)} %bitcast.2), custom_call_target="tpu_custom_call" | custom-call | tf_op jit(solution)/shard_map/sum_rows/pallas_call | solution.py:402
  45.5 14.5 %facet_rows.1 = f32[4,2,32,8192]{3,2,1,0:T(8,128)} custom-call(s32[1]{0:T(128)S(6)} %copy.7.column_ref, f32[4,2,32,128]{3,2,1,0:T(8,128)} %bitcast.3, bf16[32,1024,256]{2,1,0:T(8,128)(2,1)} %get-tuple-element.8.right), custom_call_target="tpu_custom_call" | custom-call | flops 6442450944 | bytes 26214400 | tf_op jit(solution)/shard_map/facet_rows/pallas_call | solution.py:248
